TPU v7x, 32 devices: a whole 2x2x4 slice. The times are simulated.
32 devices in a mesh: dp: 8 (over z, y), fsdp: 4 (over x, core).
Axes of the slice: x: 2, y: 2, z: 4, core: 2. Of those that a mesh axis runs over, the one named last changes fastest.
Arguments:
- features: bfloat16 [32, 8, 256, 128], P(('dp', 'fsdp')), may hold values from -60 to 60, as said below
- pick_index: int32 [32, 8, 2], P(('dp', 'fsdp')), may hold values from 0 to 255
- good_channel: int32 [32, 8], P(('dp', 'fsdp')), may hold values 0 or 1
- conv_weight: bfloat16 [1152, 128], P(None, 'fsdp'), may hold values from -0.1875 to 0.1875
- conv_bias: bfloat16 [1, 128], P(None, 'fsdp'), may hold values from -3 to 3
- head_weight: bfloat16 [2, 128], P(None, 'fsdp'), may hold values from -0.5 to 0.5
- head_bias: float32 [2], replicated, may hold values from -2 to 2
Outputs:
- grad_conv_weight: float32 [1152, 128], P('dp', 'fsdp')
- grad_conv_bias: float32 [1, 128], P(None, 'fsdp')
- grad_head_weight: float32 [2, 128], P(None, 'fsdp')
- grad_head_bias: float32 [2], replicated
- grad_features: bfloat16 [32, 8, 256, 128], P(('dp', 'fsdp'))
Inputs may be any that keep to these rules, and one draw needn't show every extreme that they name: `features`: real-valued feature maps.
All inputs are finite; a program needn't handle non-finite values. No bound on the sum of `good_channel` on one device may be relied on, other than what follows from the above.
Results may differ from a plain program's by a relative error of at most 0.007.
Values may be sent and summed in bfloat16 or wider, within the bound.
A program may use at most 64 MiB of HBM per device.

v0:
```python
import jax
import jax.numpy as jnp
from jax import lax
from jax.sharding import PartitionSpec as P

SIGMA = 20


def local_grads(features, pick_index, good_channel, conv_weight, conv_bias, head_weight, head_bias):
    patch_count, row_count, sample_count, width = features.shape
    cells = patch_count * row_count * sample_count
    padded = jnp.pad(features, ((0, 0), (1, 1), (1, 1), (0, 0)))
    preact = jnp.zeros((cells, width), jnp.float32) + conv_bias.astype(jnp.float32)
    shifted = []
    for tap_index in range(9):
        offset_row = tap_index // 3
        offset_col = tap_index % 3
        window = padded[
            :, offset_row : offset_row + row_count, offset_col : offset_col + sample_count, :
        ].reshape(cells, width)
        shifted.append(window)
        preact = preact + jnp.dot(
            window,
            conv_weight[tap_index * width : (tap_index + 1) * width],
            preferred_element_type=jnp.float32,
        )
    gate_value = jax.nn.sigmoid(preact)
    hidden = (preact * gate_value).astype(jnp.bfloat16)
    slope_term = gate_value * (1.0 + preact * (1.0 - gate_value))
    logits = (
        jnp.einsum("kc,nc->kn", head_weight, hidden, preferred_element_type=jnp.float32)
        + head_bias[:, None]
    )
    positions = jnp.arange(sample_count, dtype=jnp.float32)
    arrival = jnp.transpose(pick_index, (2, 0, 1)).astype(jnp.float32)[..., None]
    target = jnp.exp(-((positions - arrival) ** 2) / (2.0 * SIGMA * SIGMA)).reshape(2, cells)
    usable = jnp.broadcast_to(
        good_channel.astype(jnp.float32)[:, :, None], (patch_count, row_count, sample_count)
    ).reshape(1, cells)
    dlogit = (usable * (jax.nn.sigmoid(logits) - target)).astype(jnp.bfloat16)
    grad_head_weight = jnp.dot(dlogit, hidden, preferred_element_type=jnp.float32)
    grad_head_bias = jnp.sum(dlogit.astype(jnp.float32), axis=1)
    dact = jnp.einsum("kn,kc->nc", dlogit, head_weight, preferred_element_type=jnp.float32)
    dpre = (dact * slope_term).astype(jnp.bfloat16)
    grad_conv_bias = jnp.sum(dpre.astype(jnp.float32), axis=0)[None, :]
    blocks = [
        jnp.einsum("nc,nd->cd", window, dpre, preferred_element_type=jnp.float32)
        for window in shifted
    ]
    grad_conv_weight = jnp.concatenate(blocks, axis=0)
    dpad = jnp.pad(
        dpre.reshape(patch_count, row_count, sample_count, width), ((0, 0), (1, 1), (1, 1), (0, 0))
    )
    back = jnp.zeros((cells, width), jnp.float32)
    for tap_index in range(9):
        offset_row = tap_index // 3
        offset_col = tap_index % 3
        window = dpad[
            :,
            2 - offset_row : 2 - offset_row + row_count,
            2 - offset_col : 2 - offset_col + sample_count,
            :,
        ].reshape(cells, width)
        back = back + jnp.einsum(
            "nd,cd->nc",
            window,
            conv_weight[tap_index * width : (tap_index + 1) * width],
            preferred_element_type=jnp.float32,
        )
    grad_features = back.astype(jnp.bfloat16).reshape(patch_count, row_count, sample_count, width)
    return (grad_conv_weight, grad_conv_bias, grad_head_weight, grad_head_bias, grad_features)


def on_device(features, pick_index, good_channel, conv_weight, conv_bias, head_weight, head_bias):
    full_conv, full_bias, full_head = (
        lax.all_gather(conv_weight, "fsdp", axis=1, tiled=True),
        lax.all_gather(conv_bias, "fsdp", axis=1, tiled=True),
        lax.all_gather(head_weight, "fsdp", axis=1, tiled=True),
    )
    grad_kernel, grad_bias, grad_head, grad_hbias, grad_features = local_grads(
        features, pick_index, good_channel, full_conv, full_bias, full_head, head_bias
    )
    owned = lax.psum_scatter(grad_kernel, "dp", scatter_dimension=0, tiled=True)
    owned = lax.psum_scatter(owned, "fsdp", scatter_dimension=1, tiled=True)
    summed = lax.psum((grad_bias, grad_head, grad_hbias), "dp")
    bias_part, head_part = (
        lax.psum_scatter(summed[0], "fsdp", scatter_dimension=1, tiled=True),
        lax.psum_scatter(summed[1], "fsdp", scatter_dimension=1, tiled=True),
    )
    hbias_total = lax.psum(summed[2], "fsdp")
    return (owned, bias_part, head_part, hbias_total, grad_features)


def solution(mesh):
    return jax.shard_map(
        on_device,
        mesh=mesh,
        in_specs=(
            P(("dp", "fsdp"), None, None, None),
            P(("dp", "fsdp"), None, None),
            P(("dp", "fsdp"), None),
            P(None, "fsdp"),
            P(None, "fsdp"),
            P(None, "fsdp"),
            P(),
        ),
        out_specs=(
            P("dp", "fsdp"),
            P(None, "fsdp"),
            P(None, "fsdp"),
            P(),
            P(("dp", "fsdp"), None, None, None),
        ),
        check_vma=False,
    )
```

profile of v0, /device:TPU:0, one launch (start us, length us, event | category | flops | bytes accessed | tf_op | source)
XLA Modules:
  0.0 184.8 jit_solution(14172446390495054646)
XLA Ops:
  7.3 0.7 convert_bitcast_fusion.1
  7.9 0.6 dynamic-slice
  9.2 0.9 dynamic-update-slice
  10.0 8.3 %all-reduce.2 = bf16[128]{0:T(256)(128)(2,1)S(1)} all-reduce(bf16[128]{0:T(256)(128)(2,1)S(1)} %dynamic-update-slice), channel_id=1, replica_groups=mesh['dp'=8,'fsdp'=4] {'fsdp'}, use_global_device_ids=true, to_apply=%add.2 | all-reduce | flops 128 | bytes 512
  18.3 0.7 convert_bitcast_fusion
  19.0 5.2 %all-gather = bf16[4,32,2]{1,2,0:T(2,128)(2,1)S(1)} all-gather(bf16[1,32,2]{1,2,0:T(2,128)(2,1)} %bitcast.139), channel_id=1, replica_groups=mesh['dp'=8,'fsdp'=4] {'fsdp'}, dimensions={0}, use_global_device_ids=true | all-gather | bytes 640 | tf_op jit(solution)/shard_map/all_gather | solution.py:78
  24.5 6.0 %all_gather.10 = bf16[1152,128]{0,1:T(8,128)(2,1)S(1)} all-gather(bf16[1152,32]{0,1:T(8,128)(2,1)S(1)} %copy-done.2), channel_id=1, replica_groups=mesh['dp'=8,'fsdp'=4] {'fsdp'}, dimensions={1}, use_global_device_ids=true | all-gather | bytes 368640 | tf_op jit(solution)/shard_map/all_gather | solution.py:76
  30.5 3.5 %pad_slice_fusion.8 = (bf16[1,8,256,128]{3,2,1,0:T(8,128)(2,1)S(1)}, bf16[1,8,256,128]{3,2,1,0:T(8,128)(2,1)S(1)}, bf16[1,8,256,128]{3,2,1,0:T(8,128)(2,1)S(1)},...) fusion(bf16[1,8,256,128]{3,2,1,0:T(8,128)(2,1)} %param.7), kind=kLoop, calls=%fused_computation.51 | loop fusion | bytes 4718592 | tf_op jit(solution)/shard_map/slice | solution.py:18
  33.9 0.3 convolution_add_fusion.16
  34.2 0.3 convolution_add_fusion.15
  34.5 0.3 convolution_add_fusion.14
  34.9 0.3 convolution_add_fusion.13
  35.2 0.7 copy-done
  35.9 0.3 convolution_add_fusion.12
  36.2 0.3 convolution_add_fusion.11
  36.5 0.3 convolution_add_fusion.10
  36.8 0.3 convolution_add_fusion.9
  37.1 0.5 multiply_convert_fusion
  37.6 0.6 copy-done.3
  38.2 0.4 convert_reduce_fusion.1
  38.6 0.6 convert_reduce_fusion
  39.2 0.3 convolution_dynamic-update-slice_fusion.7
  39.5 0.3 convolution_dynamic-update-slice_fusion.6
  39.9 0.3 convolution_dynamic-update-slice_fusion.5
  40.2 0.3 convolution_dynamic-update-slice_fusion.4
  40.6 0.3 fusion.10
  40.9 0.3 convolution_dynamic-update-slice_fusion.3
  41.2 0.3 convolution_dynamic-update-slice_fusion.2
  41.6 0.3 convolution_dynamic-update-slice_fusion.1
  41.9 0.3 convolution_dynamic-update-slice_fusion
  42.3 0.8 copy-done.1
  43.2 0.7 copy.19
  44.0 1.0 convolution_bitcast_fusion.1
  45.0 0.8 pad_slice_fusion
  46.1 0.3 convolution_add_fusion.7
  46.4 0.3 convolution_add_fusion.6
  46.7 0.3 convolution_add_fusion.5
  47.0 0.3 convolution_add_fusion.4
  47.3 0.3 convolution_add_fusion.3
  48.1 58.1 %reduce-scatter.11.cloned.1.call-done = f32[144,128]{1,0:T(8,128)} async-done(((f32[1152,128]{1,0:T(8,128)}), f32[144,128]{1,0:T(8,128)}) %reduce-scatter.11.cloned.1.call-update) | async-done | bytes 73744 | tf_op jit(solution)/shard_map/reduce_scatter | solution.py:83
  106.2 1.6 copy.17
  107.9 1.1 fusion.1
  108.9 18.3 %reduce-scatter.15.cloned.1.call-done = f32[32,1]{1,0:T(8,128)} async-done(((f32[128,1]{1,0:T(8,128)}), f32[32,1]{1,0:T(8,128)}) %reduce-scatter.15.cloned.1.call-update) | async-done | bytes 144
  127.2 0.8 copy.20
  128.0 21.1 %reduce-scatter.17.cloned.1.call-done = f32[32,2]{1,0:T(8,128)} async-done(((f32[128,2]{1,0:T(8,128)}), f32[32,2]{1,0:T(8,128)}) %reduce-scatter.17.cloned.1.call-update) | async-done | bytes 272
  149.1 0.8 copy.22
  149.9 21.9 %all-reduce.3 = (f32[1,32]{1,0:T(1,128)}, f32[2,32]{1,0:T(2,128)}, f32[2]{0:T(128)S(1)}) all-reduce(f32[1,32]{1,0:T(1,128)S(1)} %copy.20, f32[2,32]{1,0:T(2,128)S(1)} %copy.22, f32[2]{0:T(128)S(1)} %get-tuple-element.43), channel_id=1, replica_groups=mesh['dp'=8,'fsdp'=4] {'dp'}, use_global_device_ids=true, to_apply=%region_3.4 | all-reduce | flops 98 | bytes 784 | tf_op jit(solution)/shard_map/psum | solution.py:85
  171.8 6.4 %psum.31 = f32[2]{0:T(128)} all-reduce(f32[2]{0:T(128)S(1)} %get-tuple-element.22), channel_id=1, replica_groups=mesh['dp'=8,'fsdp'=4] {'fsdp'}, use_global_device_ids=true, to_apply=%region_9.10 | all-reduce | flops 2 | bytes 16 | tf_op jit(solution)/shard_map/psum | solution.py:90
  (29 shorter events, 1.4 us)
Async XLA Ops:
  7.2 0.8 copy-start.4
  7.2 17.3 %copy-start.2 = (bf16[1152,32]{0,1:T(8,128)(2,1)S(1)}, bf16[1152,32]{0,1:T(8,128)(2,1)}, u32[]{:S(2)}) copy-start(bf16[1152,32]{0,1:T(8,128)(2,1)} %param.10) | copy-start | bytes 221188
  7.2 99.0 %reduce-scatter.11.cloned.1.call-start = ((), (), s32[]{:S(2)}) async-start(), calls=%async_computation.4 | async-start | bytes 663552 | tf_op jit(solution)/shard_map/reduce_scatter | solution.py:83
  34.8 1.0 copy-start
  37.6 0.7 copy-start.3
  42.3 0.8 copy-start.1
  43.1 84.1 %reduce-scatter.15.cloned.1.call-start = ((), (), s32[]{:S(2)}) async-start(), calls=%async_computation.6 | async-start | bytes 81920
  43.9 105.2 %reduce-scatter.17.cloned.1.call-start = ((), (), s32[]{:S(2)}) async-start(), calls=%async_computation.7 | async-start | bytes 81920
  45.0 133.3 %reduce-scatter.13.cloned.1.call-start = ((), (), s32[]{:S(2)}) async-start(), calls=%async_computation.5 | async-start | bytes 163840
Sparse Core Ops, SparseCore 0:
  43.2 62.9 reduce-scatter.10
  108.8 18.4 reduce-scatter.14
  129.7 19.3 reduce-scatter.16
  152.1 19.5 reduce-scatter.12
where the time goes:
time: 185 us
  waiting for transfers between devices  97.5 us (53%)
  blocking collectives  47.8 us (26%)
  between operations  14.7 us (8%)
  local copies, waits for them, and re-layouts  12.1 us (7%)
  matrix products  11.1 us (6%)
    reduce_scatter x1, waiting for transfers between devices, on_device(): owned = lax.psum_scatter(grad_kernel, 'dp', scatter_dimension=0, tiled=True)  58.1 us
    unnamed x7, waiting for transfers between devices  39.4 us
    psum x1, blocking collectives, on_device(): summed = lax.psum((grad_bias, grad_head, grad_hbias), 'dp')  21.9 us
    unnamed x1, blocking collectives  8.31 us
    unnamed x24, local copies, waits for them, and re-layouts  7.84 us
    psum x1, blocking collectives, on_device(): hbias_total = lax.psum(summed[2], 'fsdp')  6.4 us
    all_gather x1, blocking collectives, on_device(): lax.all_gather(conv_weight, 'fsdp', axis=1, tiled=True)  6 us
    all_gather x1, blocking collectives, on_device(): lax.all_gather(head_weight, 'fsdp', axis=1, tiled=True)  5.16 us
  transfers between devices with their start and end apart: 4, of which 3 were waited for; matrix products, arithmetic and copies ran while one was open for 5% of the time, Pallas kernels for 0%

commit v1 on v0

v1 whole, which is shorter than its diff:
```python
import functools

import jax
import jax.numpy as jnp
from jax import lax
from jax.experimental import pallas as pl
from jax.experimental.pallas import tpu as pltpu
from jax.sharding import PartitionSpec as P

SIGMA = 20
MESH = pl.DeviceIdType.MESH
AUX = 8
NT = (((1,), (1,)), ((), ()))
TN = (((0,), (0,)), ((), ()))
f32 = jnp.float32
bf16 = jnp.bfloat16


def kernel(
    n_dp,
    n_fsdp,
    rows,
    samples,
    owned,
    span,
    feat_ref,
    pick_ref,
    good_ref,
    cw_ref,
    cb_ref,
    hw_ref,
    hb_ref,
    gw_ref,
    gb_ref,
    gh_ref,
    ghb_ref,
    gf_ref,
    wt,
    wn,
    wb,
    nat,
    xc,
    dc,
    dt,
    gs,
    recv1,
    acc,
    s2,
    recv2,
    g_send,
    g_recv,
    r1_send,
    r1_recv,
    r2_send,
    r2_recv,
):
    C = wt.shape[0]
    K3 = 3 * C
    own = C // n_fsdp
    cells = rows * samples
    my_d = lax.axis_index("dp")
    my_f = lax.axis_index("fsdp")
    chunks = [(K3 * a, K3) for a in range(3)] + [(3 * K3, C)]
    mine = pl.ds(pl.multiple_of(my_f * own, own), own)

    barrier = pltpu.get_barrier_semaphore()
    for k in range(1, n_fsdp):
        pl.semaphore_signal(
            barrier, inc=1, device_id=(my_d, lax.rem(my_f + k, n_fsdp)), device_id_type=MESH
        )
    for k in range(1, n_dp):
        pl.semaphore_signal(
            barrier, inc=1, device_id=(lax.rem(my_d + k, n_dp), my_f), device_id_type=MESH
        )

    nat[...] = jnp.zeros_like(nat)
    nat[0:2, 0:own] = hw_ref[...].astype(f32)
    nat[2:3, 0:own] = cb_ref[...].astype(f32)
    wt[mine, 0 : 3 * K3] = cw_ref[...]
    wt[mine, 3 * K3 : 3 * K3 + C] = jnp.transpose(nat[...])[0:own, :].astype(bf16)

    pl.semaphore_wait(barrier, (n_fsdp - 1) + (n_dp - 1))

    gathers = []
    for q in (3, 0, 1, 2):
        start, size = chunks[q]
        for k in range(1, n_fsdp):
            copy = pltpu.make_async_remote_copy(
                src_ref=wt.at[mine, pl.ds(start, size)],
                dst_ref=wt.at[mine, pl.ds(start, size)],
                send_sem=g_send.at[k - 1, q],
                recv_sem=g_recv.at[k - 1, q],
                device_id=(my_d, lax.rem(my_f + k, n_fsdp)),
                device_id_type=MESH,
            )
            copy.start()
            gathers.append(copy)

    pad = jnp.zeros((samples, K3), bf16)
    for ref in (xc, dc):
        ref[0:samples, :] = pad
        ref[(rows + 1) * samples : (rows + 2) * samples, :] = pad
    spot = lax.broadcasted_iota(jnp.int32, (samples, C), 0)
    for i in range(rows):
        at = slice((i + 1) * samples, (i + 2) * samples)
        block = feat_ref[i * samples : (i + 1) * samples, :]
        wide = block.astype(f32)
        before = jnp.where(spot == 0, 0.0, pltpu.roll(wide, 1, 0))
        after = jnp.where(spot == samples - 1, 0.0, pltpu.roll(wide, samples - 1, 0))
        xc[at, 0:C] = before.astype(bf16)
        xc[at, C : 2 * C] = block
        xc[at, 2 * C : K3] = after.astype(bf16)

    for copy in gathers:
        copy.wait_recv()

    for t in range(9):
        part = wt[:, t * C : (t + 1) * C]
        wb[t * C : (t + 1) * C, :] = part
        wn[t * C : (t + 1) * C, :] = jnp.transpose(part.astype(f32)).astype(bf16)
    small = jnp.transpose(wt[:, 3 * K3 : 3 * K3 + C].astype(f32))
    head = small[0:16].astype(bf16)
    bias = small[2:3]

    sub = lax.broadcasted_iota(jnp.int32, (16, samples), 0)
    lane = lax.broadcasted_iota(jnp.int32, (16, samples), 1).astype(f32)
    head_bias = jnp.where(sub == 0, hb_ref[0], hb_ref[1])
    grad_head = jnp.zeros((16, C), f32)
    grad_hbias = jnp.zeros((16, samples), f32)
    grad_bias = jnp.zeros((1, C), f32)
    for i in range(rows):
        preact = bias
        for a in range(3):
            preact = preact + jnp.dot(
                xc[(i + a) * samples : (i + a + 1) * samples, :],
                wn[a * K3 : (a + 1) * K3, :],
                preferred_element_type=f32,
            )
        gate = jax.nn.sigmoid(preact)
        hidden = (preact * gate).astype(bf16)
        slope = gate * (1.0 + preact * (1.0 - gate))
        logits = lax.dot_general(head, hidden, NT, preferred_element_type=f32) + head_bias
        arrival = jnp.where(sub == 0, pick_ref[0, i], pick_ref[1, i]).astype(f32)
        gap = lane - arrival
        target = jnp.exp(-(gap * gap) / (2.0 * SIGMA * SIGMA))
        usable = jnp.where(sub < 2, good_ref[0, i].astype(f32), 0.0)
        dlogit = (usable * (jax.nn.sigmoid(logits) - target)).astype(bf16)
        grad_head = grad_head + jnp.dot(dlogit, hidden, preferred_element_type=f32)
        grad_hbias = grad_hbias + dlogit.astype(f32)
        dact = lax.dot_general(dlogit, head, TN, preferred_element_type=f32)
        dpre = (dact * slope).astype(bf16)
        wide = dpre.astype(f32)
        grad_bias = grad_bias + jnp.sum(wide, axis=0, keepdims=True)
        dt[:, i * samples : (i + 1) * samples] = jnp.transpose(wide).astype(bf16)
        before = jnp.where(spot == 0, 0.0, pltpu.roll(wide, 1, 0))
        after = jnp.where(spot == samples - 1, 0.0, pltpu.roll(wide, samples - 1, 0))
        at = slice((i + 1) * samples, (i + 2) * samples)
        dc[at, 0:C] = after.astype(bf16)
        dc[at, C : 2 * C] = dpre
        dc[at, 2 * C : K3] = before.astype(bf16)

    def scatter(q):
        start, size = chunks[q]
        for k in range(1, n_fsdp):
            peer = lax.rem(my_f + k, n_fsdp)
            copy = pltpu.make_async_remote_copy(
                src_ref=gs.at[pl.ds(pl.multiple_of(peer * own, own), own), pl.ds(start, size)],
                dst_ref=recv1.at[k - 1, :, pl.ds(start, size)],
                send_sem=r1_send.at[k - 1, q],
                recv_sem=r1_recv.at[k - 1, q],
                device_id=(my_d, peer),
                device_id_type=MESH,
            )
            copy.start()
            firsts[q].append(copy)

    def split(value):
        high = value.astype(bf16).astype(f32)
        return high, value - high

    firsts = [[], [], [], []]
    for a in range(3):
        grads = jnp.dot(
            dt[...], xc[a * samples : a * samples + cells, :], preferred_element_type=f32
        )
        gs[:, a * K3 : (a + 1) * K3] = grads.astype(bf16)
        scatter(a)
    hsum = jnp.sum(grad_hbias, axis=1, keepdims=True)
    sub8 = lax.broadcasted_iota(jnp.int32, (AUX, C), 0)
    rest = jnp.where(sub8 == 2, grad_bias, jnp.where(sub8 == 3, hsum[0:1], hsum[1:2]))
    rest = jnp.where(sub8 < 2, grad_head[0:AUX], jnp.where(sub8 < 5, rest, 0.0))
    high, low = split(rest)
    nat[...] = jnp.zeros_like(nat)
    nat[0:AUX, :] = high
    nat[AUX : 2 * AUX, :] = low
    gs[:, 3 * K3 : 3 * K3 + C] = jnp.transpose(nat[...]).astype(bf16)
    scatter(3)

    for i in range(rows):
        back = jnp.zeros((samples, C), f32)
        for a in range(3):
            back = back + jnp.dot(
                dc[(i + 2 - a) * samples : (i + 3 - a) * samples, :],
                wb[a * K3 : (a + 1) * K3, :],
                preferred_element_type=f32,
            )
        gf_ref[i * samples : (i + 1) * samples, :] = back.astype(bf16)

    for q in range(4):
        start, size = chunks[q]
        total = gs[mine, start : start + size].astype(f32)
        for k in range(1, n_fsdp):
            firsts[q][k - 1].wait_recv()
            total = total + recv1[k - 1, :, start : start + size].astype(f32)
        acc[:, start : start + size] = total
    acc[:, 3 * K3 + C :] = jnp.zeros((own, acc.shape[1] - 3 * K3 - C), f32)

    column = lax.broadcasted_iota(jnp.int32, (own, span), 1)
    small = acc[:, 3 * K3 : 3 * K3 + span]
    small = small + pltpu.roll(small, span - AUX, 1)
    high, low = split(small)
    high = pltpu.roll(high, owned, 1)
    low = pltpu.roll(low, owned + AUX, 1)
    small = jnp.where(column < owned + AUX, high, jnp.where(column < owned + 2 * AUX, low, 0.0))
    for d in range(n_dp):
        base = owned * d // 128 * 128
        piece = acc[:, base : base + span + 128]
        if owned * d > base:
            piece = pltpu.roll(piece, span + 128 - (owned * d - base), 1)
        s2[d] = jnp.where(column < owned, piece[:, 0:span], small).astype(bf16)

    seconds = []
    for k in range(1, n_dp):
        peer = lax.rem(my_d + k, n_dp)
        copy = pltpu.make_async_remote_copy(
            src_ref=s2.at[peer],
            dst_ref=recv2.at[k - 1],
            send_sem=r2_send.at[k - 1],
            recv_sem=r2_recv.at[k - 1],
            device_id=(peer, my_f),
            device_id_type=MESH,
        )
        copy.start()
        seconds.append(copy)
    total = s2[my_d].astype(f32)
    for k in range(1, n_dp):
        seconds[k - 1].wait_recv()
        total = total + recv2[k - 1].astype(f32)
    gw_ref[...] = total[:, 0:owned]
    small = pltpu.roll(total, span - owned, 1)
    small = small + pltpu.roll(small, span - AUX, 1)
    nat[0:own, :] = small[:, 0:C]
    ghb_ref[...] = small[0:1, 3:5]
    turned = jnp.transpose(nat[...])
    gh_ref[...] = turned[0:2, 0:own]
    gb_ref[...] = turned[2:3, 0:own]

    for copies in [gathers, *firsts, seconds]:
        for copy in copies:
            copy.wait_send()


def on_device(n_dp, n_fsdp, features, pick_index, good_channel, conv_weight, conv_bias, head_weight, head_bias):
    _, rows, samples, C = features.shape
    cells = rows * samples
    K9 = conv_weight.shape[0]
    own = conv_weight.shape[1]
    owned = K9 // n_dp
    span = -(-(owned + 2 * AUX) // 128) * 128
    vmem = pl.BlockSpec(memory_space=pltpu.VMEM)
    smem = pl.BlockSpec(memory_space=pltpu.SMEM)
    dma = pltpu.SemaphoreType.DMA
    gw, gb, gh, ghb, gf = pl.pallas_call(
        functools.partial(kernel, n_dp, n_fsdp, rows, samples, owned, span),
        out_shape=(
            jax.ShapeDtypeStruct((own, owned), f32),
            jax.ShapeDtypeStruct((1, own), f32),
            jax.ShapeDtypeStruct((2, own), f32),
            jax.ShapeDtypeStruct((1, 2), f32),
            jax.ShapeDtypeStruct((cells, C), bf16),
        ),
        in_specs=[vmem, smem, smem, vmem, vmem, vmem, smem],
        out_specs=(vmem,) * 5,
        scratch_shapes=[
            pltpu.VMEM((C, K9 + C), bf16),
            pltpu.VMEM((K9, C), bf16),
            pltpu.VMEM((K9, C), bf16),
            pltpu.VMEM((C, C), f32),
            pltpu.VMEM(((rows + 2) * samples, 3 * C), bf16),
            pltpu.VMEM(((rows + 2) * samples, 3 * C), bf16),
            pltpu.VMEM((C, cells), bf16),
            pltpu.VMEM((C, K9 + C), bf16),
            pltpu.VMEM((n_fsdp - 1, own, K9 + C), bf16),
            pltpu.VMEM((own, K9 + span + 128), f32),
            pltpu.VMEM((n_dp, own, span), bf16),
            pltpu.VMEM((n_dp - 1, own, span), bf16),
            dma((n_fsdp - 1, 4)),
            dma((n_fsdp - 1, 4)),
            dma((n_fsdp - 1, 4)),
            dma((n_fsdp - 1, 4)),
            dma((n_dp - 1,)),
            dma((n_dp - 1,)),
        ],
        compiler_params=pltpu.CompilerParams(
            collective_id=0, has_side_effects=True, vmem_limit_bytes=48 * 1024 * 1024
        ),
        cost_estimate=pl.CostEstimate(
            flops=6 * cells * K9 * C, bytes_accessed=4 * cells * C, transcendentals=2 * cells * C
        ),
    )(
        features.reshape(cells, C),
        jnp.transpose(pick_index[0]),
        good_channel,
        jnp.transpose(conv_weight),
        conv_bias,
        head_weight,
        head_bias,
    )
    return jnp.transpose(gw), gb, gh, ghb.reshape(2), gf.reshape(features.shape)


def solution(mesh):
    return jax.shard_map(
        functools.partial(on_device, mesh.shape["dp"], mesh.shape["fsdp"]),
        mesh=mesh,
        in_specs=(
            P(("dp", "fsdp"), None, None, None),
            P(("dp", "fsdp"), None, None),
            P(("dp", "fsdp"), None),
            P(None, "fsdp"),
            P(None, "fsdp"),
            P(None, "fsdp"),
            P(),
        ),
        out_specs=(
            P("dp", "fsdp"),
            P(None, "fsdp"),
            P(None, "fsdp"),
            P(),
            P(("dp", "fsdp"), None, None, None),
        ),
        check_vma=False,
    )
```

time: 185 us -> 33.1 us (0.18)
  waiting for transfers between devices: 97.5 us -> 0 us
  blocking collectives: 47.8 us -> 0 us
  Pallas kernels: 0 us -> 26.6 us
  between operations: 14.7 us -> 0.69 us
  matrix products: 11.1 us -> 0 us
  local copies, waits for them, and re-layouts: 12.1 us -> 5.61 us
    reduce_scatter x1 -> x0, waiting for transfers between devices: 58.1 us -> none  [on_device(): owned = lax.psum_scatter(grad_kernel, 'dp', scatter_dimension=0, tiled=True)]
    unnamed x7 -> x0, waiting for transfers between devices: 39.4 us -> none
    psum x2 -> x0, blocking collectives: 28.3 us -> none  [the longest x1 21.9 us: on_device(): summed = lax.psum((grad_bias, grad_head, grad_hbias), 'dp')]
    pallas_call x0 -> x1, Pallas kernels: none -> 26.6 us  [on_device(): pl.pallas_call(functools.partial(kernel, n_dp, n_fsdp, rows, samples, own...]
    all_gather x2 -> x0, blocking collectives: 11.2 us -> none  [the longest x1 6 us: on_device(): lax.all_gather(conv_weight, 'fsdp', axis=1, tiled=True)]
    dot_general x29 -> x0, matrix products: 10.1 us -> none  [the longest x9 3.32 us: local_grads(): jnp.einsum('nd,cd->nc', window, conv_weight[tap_index * width:(tap_index...]
    unnamed x1 -> x0, blocking collectives: 8.31 us -> none
    slice x2 -> x0, local copies, waits for them, and re-layouts: 4.29 us -> none  [the longest x1 3.48 us: local_grads(): padded[:, offset_row:offset_row + row_count, offset_col:offset_col + samp...]
  transfers between devices with their start and end apart: 4 -> 0, of which waited for: 3 -> 0; matrix products, arithmetic and copies ran while one was open for 5% -> 0% of each run, Pallas kernels for 0% -> 0%
where the time goes in v1:
time: 33.1 us; the launch traced here: 32.9 us
  Pallas kernels  26.6 us (80%)
  local copies, waits for them, and re-layouts  5.61 us (17%)
  between operations  0.69 us (2%)
    pallas_call x1, Pallas kernels, on_device(): pl.pallas_call(functools.partial(kernel, n_dp, n_fsdp, rows, samples, own...  26.6 us
    unnamed x19, local copies, waits for them, and re-layouts  5.61 us

profile of v1, /device:TPU:0, one launch (start us, length us, event | category | flops | bytes accessed | tf_op | source)
XLA Modules:
  0.0 32.9 jit_solution(11601310553173020003)
XLA Ops:
  0.6 0.0 copy-start.4
  0.6 0.0 copy-start.5
  0.7 0.0 copy-start.6
  0.7 0.0 copy-start.2
  0.7 0.0 copy-start.3
  0.7 0.6 %copy-done.4 = bf16[1,32]{1,0:T(2,128)(2,1)S(1)} copy-done((bf16[1,32]{1,0:T(2,128)(2,1)S(1)}, bf16[1,32]{1,0:T(2,128)(2,1)}, u32[]{:S(2)}) %copy-start.4) | copy-done | bytes 88
  1.3 0.0 copy-done.5
  1.3 0.0 copy-done.6
  1.3 0.0 copy-done.2
  1.4 0.0 copy-done.3
  1.4 0.0 copy-start
  1.4 1.0 %copy-done = bf16[1,8,256,128]{3,2,1,0:T(8,128)(2,1)S(1)} copy-done((bf16[1,8,256,128]{3,2,1,0:T(8,128)(2,1)S(1)}, bf16[1,8,256,128]{3,2,1,0:T(8,128)(2,1)}, u32[]{:S(2)}) %copy-start) | copy-done | bytes 524312
  2.4 0.0 copy-start.1
  2.4 0.9 %copy-done.1 = bf16[1152,32]{0,1:T(8,128)(2,1)S(1)} copy-done((bf16[1152,32]{0,1:T(8,128)(2,1)S(1)}, bf16[1152,32]{0,1:T(8,128)(2,1)}, u32[]{:S(2)}) %copy-start.1) | copy-done | bytes 73752
  3.3 26.6 %shard_map.110 = (f32[32,144]{1,0:T(8,128)S(1)}, f32[1,32]{1,0:T(1,128)S(1)}, f32[2,32]{1,0:T(2,128)S(1)}, f32[1,2]{1,0:T(1,128)S(1)}, bf16[2048,128]{1,0:T(8,128)(2,1)S(1)}) custom-call(bf16[2048,128]{1,0:T(8,128)(2,1)S(1)} %bitcast.10, s32[2,8]{1,0:T(2,128)S(1)} %bitcast.12, s32[1,8]{1,0:T(1,128)S(1)} %copy-done.3, bf16[32,1152]{1,0:T(8,128)(2,1)S(1)} %bitcast.11, ...), custom_call_target="tpu_custom_call" | custom-call | flops 1811939328 | bytes 1048576 | tf_op jit(solution)/shard_map/pallas_call | solution.py:273
  29.9 0.6 %copy.17 = f32[144,32]{0,1:T(8,128)} copy(f32[144,32]{0,1:T(8,128)S(1)} %bitcast.9) | data formatting | bytes 36864
  30.5 0.5 %copy.18 = f32[1,32]{1,0:T(1,128)} copy(f32[1,32]{1,0:T(1,128)S(1)} %get-tuple-element.21) | data formatting | bytes 256
  31.0 0.6 %copy.19 = f32[2,32]{1,0:T(2,128)} copy(f32[2,32]{1,0:T(2,128)S(1)} %get-tuple-element.22) | data formatting | bytes 512
  31.6 0.5 %copy.20 = f32[2]{0:T(128)} copy(f32[2]{0:T(128)S(1)} %bitcast.13) | data formatting | bytes 16
  32.1 0.8 %copy.21 = bf16[1,8,256,128]{3,2,1,0:T(8,128)(2,1)} copy(bf16[1,8,256,128]{3,2,1,0:T(8,128)(2,1)S(1)} %bitcast.8) | data formatting | bytes 1048576
Async XLA Ops:
  0.6 0.7 %copy-start.4 = (bf16[1,32]{1,0:T(2,128)(2,1)S(1)}, bf16[1,32]{1,0:T(2,128)(2,1)}, u32[]{:S(2)}) copy-start(bf16[1,32]{1,0:T(2,128)(2,1)} %cb_ref.1) | copy-start | bytes 196
  0.6 0.7 %copy-start.5 = (bf16[2,32]{1,0:T(2,128)(2,1)S(1)}, bf16[2,32]{1,0:T(2,128)(2,1)}, u32[]{:S(2)}) copy-start(bf16[2,32]{1,0:T(2,128)(2,1)} %hw_ref.1) | copy-start | bytes 388
  0.7 0.7 %copy-start.6 = (f32[2]{0:T(128)S(1)}, f32[2]{0:T(128)}, u32[]{:S(2)}) copy-start(f32[2]{0:T(128)} %hb_ref.1) | copy-start | bytes 28
  0.7 0.7 %copy-start.2 = (s32[1,8,2]{1,2,0:T(2,128)S(1)}, s32[1,8,2]{1,2,0:T(2,128)}, u32[]{:S(2)}) copy-start(s32[1,8,2]{1,2,0:T(2,128)} %param.8) | copy-start | bytes 196
  0.7 0.7 %copy-start.3 = (s32[1,8]{1,0:T(1,128)S(1)}, s32[1,8]{1,0:T(1,128)}, u32[]{:S(2)}) copy-start(s32[1,8]{1,0:T(1,128)} %good_ref.1) | copy-start | bytes 100
  1.4 1.0 %copy-start = (bf16[1,8,256,128]{3,2,1,0:T(8,128)(2,1)S(1)}, bf16[1,8,256,128]{3,2,1,0:T(8,128)(2,1)}, u32[]{:S(2)}) copy-start(bf16[1,8,256,128]{3,2,1,0:T(8,128)(2,1)} %param.7) | copy-start | bytes 1572868
  2.4 0.9 %copy-start.1 = (bf16[1152,32]{0,1:T(8,128)(2,1)S(1)}, bf16[1152,32]{0,1:T(8,128)(2,1)}, u32[]{:S(2)}) copy-start(bf16[1152,32]{0,1:T(8,128)(2,1)} %param.10) | copy-start | bytes 221188

commit v2 on v1

v2 whole, which is shorter than its diff:
```python
import functools

import jax
import jax.numpy as jnp
from jax import lax
from jax.experimental import pallas as pl
from jax.experimental.pallas import tpu as pltpu
from jax.sharding import PartitionSpec as P

SIGMA = 20
MESH = pl.DeviceIdType.MESH
AUX = 8
NT = (((1,), (1,)), ((), ()))
TN = (((0,), (0,)), ((), ()))
f32 = jnp.float32
bf16 = jnp.bfloat16


def kernel(
    n_dp,
    n_fsdp,
    rows,
    samples,
    owned,
    span,
    feat_ref,
    pick_ref,
    good_ref,
    cw_ref,
    cb_ref,
    hw_ref,
    hb_ref,
    gw_ref,
    gb_ref,
    gh_ref,
    ghb_ref,
    gf_ref,
    feat,
    wt,
    wn,
    wb,
    nat,
    xc,
    dc,
    dt,
    pre,
    gs,
    recv_a,
    send_b,
    recv_b,
    acc,
    s2,
    recv2,
    load,
    g_send,
    g_recv,
    a_send,
    a_recv,
    b_send,
    b_recv,
    r2_send,
    r2_recv,
):
    C = wt.shape[0]
    K3 = 3 * C
    K9 = 9 * C
    own = C // n_fsdp
    cells = rows * samples
    my_d = lax.axis_index("dp")
    my_f = lax.axis_index("fsdp")
    twin = my_f + 1 - 2 * lax.rem(my_f, 2)
    across = lax.rem(my_f + 2, 4)
    twin_across = lax.rem(twin + 2, 4)
    chunks = [pl.ds(0, K3), pl.ds(K3, K3), pl.ds(2 * K3, K3 + C)]

    def rows_of(f):
        return pl.ds(pl.multiple_of(f * own, own), own)

    mine = rows_of(my_f)

    def send(src, dst, send_sem, recv_sem, peer):
        copy = pltpu.make_async_remote_copy(
            src_ref=src,
            dst_ref=dst,
            send_sem=send_sem,
            recv_sem=recv_sem,
            device_id=peer,
            device_id_type=MESH,
        )
        copy.start()
        return copy

    load_kernel = pltpu.make_async_copy(cw_ref, wt.at[mine, pl.ds(0, K9)], load.at[0])
    load_features = pltpu.make_async_copy(feat_ref, feat, load.at[1])
    load_kernel.start()
    load_features.start()

    barrier = pltpu.get_barrier_semaphore()
    for f in (twin, across):
        pl.semaphore_signal(barrier, inc=1, device_id=(my_d, f), device_id_type=MESH)
    for k in range(1, n_dp):
        pl.semaphore_signal(
            barrier, inc=1, device_id=(lax.rem(my_d + k, n_dp), my_f), device_id_type=MESH
        )

    nat[...] = jnp.zeros_like(nat)
    nat[0:2, 0:own] = hw_ref[...].astype(f32)
    nat[2:3, 0:own] = cb_ref[...].astype(f32)
    wt[mine, K9 : K9 + C] = jnp.transpose(nat[...])[0:own, :].astype(bf16)
    pad = jnp.zeros((samples, K3), bf16)
    for ref in (xc, dc):
        ref[0:samples, :] = pad
        ref[(rows + 1) * samples : (rows + 2) * samples, :] = pad
    load_kernel.wait()

    pl.semaphore_wait(barrier, 2 + (n_dp - 1))

    sent = []
    gather_x, gather_t, gather_r = [], [], []
    for q in range(3):
        part = wt.at[mine, chunks[q]]
        gather_x.append(send(part, part, g_send.at[0, q], g_recv.at[0, q], (my_d, across)))
        gather_t.append(send(part, part, g_send.at[1, q], g_recv.at[1, q], (my_d, twin)))
    load_features.wait()

    spot = lax.broadcasted_iota(jnp.int32, (samples, C), 0)

    def shifts(wide):
        before = jnp.where(spot == 0, 0.0, pltpu.roll(wide, 1, 0))
        after = jnp.where(spot == samples - 1, 0.0, pltpu.roll(wide, samples - 1, 0))
        return before.astype(bf16), after.astype(bf16)

    for i in range(rows):
        at = slice((i + 1) * samples, (i + 2) * samples)
        block = feat[i * samples : (i + 1) * samples, :]
        before, after = shifts(block.astype(f32))
        xc[at, 0:C] = before
        xc[at, C : 2 * C] = block
        xc[at, 2 * C : K3] = after

    def relay(q):
        gather_x[q].wait_recv()
        part = wt.at[rows_of(across), chunks[q]]
        gather_r.append(send(part, part, g_send.at[2, q], g_recv.at[2, q], (my_d, twin)))

    relay(0)
    for a in range(3):
        if a < 2:
            relay(a + 1)
        gather_t[a].wait_recv()
        gather_r[a].wait_recv()
        for t in range(3 * a, 3 * a + 3):
            part = wt[:, t * C : (t + 1) * C]
            wb[t * C : (t + 1) * C, :] = part
            wn[t * C : (t + 1) * C, :] = jnp.transpose(part.astype(f32)).astype(bf16)
        term = jnp.dot(
            xc[a * samples : a * samples + cells, :],
            wn[a * K3 : (a + 1) * K3, :],
            preferred_element_type=f32,
        )
        pre[...] = term if a == 0 else pre[...] + term
    small = jnp.transpose(wt[:, K9 : K9 + C].astype(f32))
    head = small[0:16].astype(bf16)
    bias = small[2:3]

    sub = lax.broadcasted_iota(jnp.int32, (16, samples), 0)
    lane = lax.broadcasted_iota(jnp.int32, (16, samples), 1).astype(f32)
    head_bias = jnp.where(sub == 0, hb_ref[0], hb_ref[1])
    grad_head = jnp.zeros((16, C), f32)
    grad_hbias = jnp.zeros((16, samples), f32)
    grad_bias = jnp.zeros((1, C), f32)
    step = 2
    for i0 in range(0, rows, step):
        cut = slice(i0 * samples, (i0 + step) * samples)
        preact = pre[cut, :] + bias
        gate = jax.nn.sigmoid(preact)
        hidden = (preact * gate).astype(bf16)
        slope = gate * (1.0 + preact * (1.0 - gate))
        logits = lax.dot_general(head, hidden, NT, preferred_element_type=f32)
        dlogits = []
        for i in range(i0, i0 + step):
            arrival = jnp.where(sub == 0, pick_ref[0, i], pick_ref[1, i]).astype(f32)
            gap = lane - arrival
            target = jnp.exp(-(gap * gap) / (2.0 * SIGMA * SIGMA))
            usable = jnp.where(sub < 2, good_ref[0, i].astype(f32), 0.0)
            here = logits[:, (i - i0) * samples : (i - i0 + 1) * samples] + head_bias
            dlogits.append((usable * (jax.nn.sigmoid(here) - target)).astype(bf16))
            grad_hbias = grad_hbias + dlogits[-1].astype(f32)
        dlogit = jnp.concatenate(dlogits, axis=1)
        grad_head = grad_head + jnp.dot(dlogit, hidden, preferred_element_type=f32)
        dact = lax.dot_general(dlogit, head, TN, preferred_element_type=f32)
        dpre = (dact * slope).astype(bf16)
        wide = dpre.astype(f32)
        grad_bias = grad_bias + jnp.sum(wide, axis=0, keepdims=True)
        dt[:, cut] = jnp.transpose(wide).astype(bf16)
        for i in range(i0, i0 + step):
            inner = slice((i - i0) * samples, (i - i0 + 1) * samples)
            before, after = shifts(wide[inner])
            at = slice((i + 1) * samples, (i + 2) * samples)
            dc[at, 0:C] = after
            dc[at, C : 2 * C] = dpre[inner]
            dc[at, 2 * C : K3] = before

    def split(value):
        high = value.astype(bf16).astype(f32)
        return high, value - high

    def resplit(value):
        lanes = lax.broadcasted_iota(jnp.int32, value.shape, 1)
        high, low = split(value + pltpu.roll(value, value.shape[1] - AUX, 1))
        low = pltpu.roll(low, AUX, 1)
        return jnp.where(lanes < AUX, high, jnp.where(lanes < 2 * AUX, low, 0.0))

    first_a, first_b = [], []

    def stage_a(q):
        first_a.append(
            [
                send(
                    gs.at[rows_of(f), chunks[q]],
                    recv_a.at[j, :, chunks[q]],
                    a_send.at[j, q],
                    a_recv.at[j, q],
                    (my_d, twin),
                )
                for j, f in ((1, twin_across), (0, twin))
            ]
        )

    def stage_b(q):
        first_a[q][0].wait_recv()
        total = gs[rows_of(across), chunks[q]].astype(f32) + recv_a[1, :, chunks[q]].astype(f32)
        if q == 2:
            send_b[:, 2 * K3 : K9] = total[:, 0:K3].astype(bf16)
            send_b[:, K9 : K9 + C] = resplit(total[:, K3:]).astype(bf16)
        else:
            send_b[:, chunks[q]] = total.astype(bf16)
        part = send_b.at[:, chunks[q]]
        first_b.append(
            send(part, recv_b.at[:, chunks[q]], b_send.at[q], b_recv.at[q], (my_d, across))
        )

    def kernel_grads(a):
        grads = jnp.dot(
            dt[...], xc[a * samples : a * samples + cells, :], preferred_element_type=f32
        )
        gs[:, a * K3 : (a + 1) * K3] = grads.astype(bf16)

    def feature_grads(i):
        back = jnp.zeros((samples, C), f32)
        for a in range(3):
            back = back + jnp.dot(
                dc[(i + 2 - a) * samples : (i + 3 - a) * samples, :],
                wb[a * K3 : (a + 1) * K3, :],
                preferred_element_type=f32,
            )
        gf_ref[i * samples : (i + 1) * samples, :] = back.astype(bf16)

    hsum = jnp.sum(grad_hbias, axis=1, keepdims=True)
    sub8 = lax.broadcasted_iota(jnp.int32, (AUX, C), 0)
    rest = jnp.where(sub8 == 2, grad_bias, jnp.where(sub8 == 3, hsum[0:1], hsum[1:2]))
    rest = jnp.where(sub8 < 2, grad_head[0:AUX], jnp.where(sub8 < 5, rest, 0.0))
    high, low = split(rest)
    nat[...] = jnp.zeros_like(nat)
    nat[0:AUX, :] = high
    nat[AUX : 2 * AUX, :] = low
    gs[:, K9 : K9 + C] = jnp.transpose(nat[...]).astype(bf16)
    kernel_grads(0)
    stage_a(0)
    kernel_grads(1)
    stage_a(1)
    stage_b(0)
    kernel_grads(2)
    stage_a(2)
    stage_b(1)
    for i in range(rows // 2):
        feature_grads(i)
    stage_b(2)
    for i in range(rows // 2, rows):
        feature_grads(i)

    for q in range(3):
        first_a[q][1].wait_recv()
        first_b[q].wait_recv()
        acc[:, chunks[q]] = (
            gs[mine, chunks[q]].astype(f32)
            + recv_a[0, :, chunks[q]].astype(f32)
            + recv_b[:, chunks[q]].astype(f32)
        )
    acc[:, K9 + C :] = jnp.zeros((own, acc.shape[1] - K9 - C), f32)

    column = lax.broadcasted_iota(jnp.int32, (own, span), 1)
    small = pltpu.roll(resplit(acc[:, K9 : K9 + span]), owned, 1)
    for d in range(n_dp):
        base = owned * d // 128 * 128
        piece = acc[:, base : base + span + 128]
        if owned * d > base:
            piece = pltpu.roll(piece, span + 128 - (owned * d - base), 1)
        piece = jnp.where(column < owned, piece[:, 0:span], small)
        s2[d, 0:own, :] = piece[:, 0:128].astype(bf16)
        if span > 128:
            more = piece[:, 128:256]
            half = own // 2
            more = jnp.where(
                column[0:half, 0:128] < 64, more[0:half], pltpu.roll(more[half:], 64, 1)
            )
            s2[d, own : own + half, :] = more.astype(bf16)

    seconds = []
    for k in range(1, n_dp):
        peer = lax.rem(my_d + k, n_dp)
        seconds.append(
            send(s2.at[peer], recv2.at[k - 1], r2_send.at[k - 1], r2_recv.at[k - 1], (peer, my_f))
        )
    total = s2[my_d].astype(f32)
    for k in range(1, n_dp):
        seconds[k - 1].wait_recv()
        total = total + recv2[k - 1].astype(f32)
    if span > 128:
        more = total[own:]
        more = jnp.concatenate([more, pltpu.roll(more, 64, 1)], axis=0)
        total = jnp.concatenate([total[0:own], more], axis=1)
    gw_ref[...] = total[:, 0:owned]
    small = pltpu.roll(total, span - owned, 1)
    small = small + pltpu.roll(small, span - AUX, 1)
    nat[0:own, :] = small[:, 0:C]
    ghb_ref[...] = small[0:1, 3:5]
    turned = jnp.transpose(nat[...])
    gh_ref[...] = turned[0:2, 0:own]
    gb_ref[...] = turned[2:3, 0:own]

    for copies in [gather_x, gather_t, gather_r, *first_a, first_b, seconds]:
        for copy in copies:
            copy.wait_send()


def store_kernel(*refs):
    count = len(refs) // 2
    copies = [
        pltpu.make_async_copy(refs[i], refs[count + i], refs[-1].at[i]) for i in range(count)
    ]
    for copy in copies:
        copy.start()
    for copy in copies:
        copy.wait()


def on_device(n_dp, n_fsdp, features, pick_index, good_channel, conv_weight, conv_bias, head_weight, head_bias):
    _, rows, samples, C = features.shape
    cells = rows * samples
    K9 = conv_weight.shape[0]
    own = conv_weight.shape[1]
    owned = K9 // n_dp
    wire = own
    span = -(-(owned + 2 * AUX) // 128) * 128
    if span > 128:
        wire = own + own // 2
    vmem = pl.BlockSpec(memory_space=pltpu.VMEM)
    anywhere = pl.BlockSpec(memory_space=pl.ANY)
    hbm = pl.BlockSpec(memory_space=pltpu.HBM)
    smem = pl.BlockSpec(memory_space=pltpu.SMEM)
    dma = pltpu.SemaphoreType.DMA
    results = pl.pallas_call(
        functools.partial(kernel, n_dp, n_fsdp, rows, samples, owned, span),
        out_shape=(
            jax.ShapeDtypeStruct((own, owned), f32),
            jax.ShapeDtypeStruct((1, own), f32),
            jax.ShapeDtypeStruct((2, own), f32),
            jax.ShapeDtypeStruct((1, 2), f32),
            jax.ShapeDtypeStruct((cells, C), bf16),
        ),
        in_specs=[hbm, smem, smem, hbm, vmem, vmem, smem],
        out_specs=(vmem,) * 5,
        scratch_shapes=[
            pltpu.VMEM((cells, C), bf16),
            pltpu.VMEM((C, K9 + C), bf16),
            pltpu.VMEM((K9, C), bf16),
            pltpu.VMEM((K9, C), bf16),
            pltpu.VMEM((C, C), f32),
            pltpu.VMEM(((rows + 2) * samples, 3 * C), bf16),
            pltpu.VMEM(((rows + 2) * samples, 3 * C), bf16),
            pltpu.VMEM((C, cells), bf16),
            pltpu.VMEM((cells, C), f32),
            pltpu.VMEM((C, K9 + C), bf16),
            pltpu.VMEM((2, own, K9 + C), bf16),
            pltpu.VMEM((own, K9 + C), bf16),
            pltpu.VMEM((own, K9 + C), bf16),
            pltpu.VMEM((own, K9 + span + 128), f32),
            pltpu.VMEM((n_dp, wire, 128), bf16),
            pltpu.VMEM((n_dp - 1, wire, 128), bf16),
            dma((2,)),
            dma((3, 3)),
            dma((3, 3)),
            dma((2, 3)),
            dma((2, 3)),
            dma((3,)),
            dma((3,)),
            dma((n_dp - 1,)),
            dma((n_dp - 1,)),
        ],
        compiler_params=pltpu.CompilerParams(
            collective_id=0, has_side_effects=True, vmem_limit_bytes=48 * 1024 * 1024
        ),
        cost_estimate=pl.CostEstimate(
            flops=6 * cells * K9 * C, bytes_accessed=4 * cells * C, transcendentals=2 * cells * C
        ),
    )(
        features.reshape(cells, C),
        jnp.transpose(pick_index[0]),
        good_channel,
        jnp.transpose(conv_weight),
        conv_bias,
        head_weight,
        head_bias,
    )
    gw, gb, gh, ghb, gf = pl.pallas_call(
        store_kernel,
        out_shape=tuple(jax.ShapeDtypeStruct(r.shape, r.dtype) for r in results),
        in_specs=[anywhere] * 5,
        out_specs=(hbm,) * 5,
        scratch_shapes=[dma((5,))],
        compiler_params=pltpu.CompilerParams(vmem_limit_bytes=1024 * 1024),
    )(*results)
    return jnp.transpose(gw), gb, gh, ghb.reshape(2), gf.reshape(features.shape)


def solution(mesh):
    return jax.shard_map(
        functools.partial(on_device, mesh.shape["dp"], mesh.shape["fsdp"]),
        mesh=mesh,
        in_specs=(
            P(("dp", "fsdp"), None, None, None),
            P(("dp", "fsdp"), None, None),
            P(("dp", "fsdp"), None),
            P(None, "fsdp"),
            P(None, "fsdp"),
            P(None, "fsdp"),
            P(),
        ),
        out_specs=(
            P("dp", "fsdp"),
            P(None, "fsdp"),
            P(None, "fsdp"),
            P(),
            P(("dp", "fsdp"), None, None, None),
        ),
        check_vma=False,
    )
```

time: 33.1 us -> 28.1 us (0.85)
  local copies, waits for them, and re-layouts: 5.61 us -> 2.61 us
  Pallas kernels: 26.6 us -> 24.6 us
    unnamed x19 -> x14, local copies, waits for them, and re-layouts: 5.61 us -> 2.61 us
    pallas_call x1, Pallas kernels: 26.6 us -> 23.7 us  [on_device(): pl.pallas_call(functools.partial(kernel, n_dp, n_fsdp, rows, samples, own...]
    pallas_call x0 -> x1, Pallas kernels: none -> 0.86 us  [on_device(): pl.pallas_call(store_kernel, out_shape=tuple((jax.ShapeDtypeStruct(r.shap...]
where the time goes in v2:
time: 28.1 us; the launch traced here: 27.9 us
  Pallas kernels  24.6 us (88%)
  local copies, waits for them, and re-layouts  2.61 us (9%)
  between operations  0.69 us (2%)
    pallas_call x1, Pallas kernels, on_device(): pl.pallas_call(functools.partial(kernel, n_dp, n_fsdp, rows, samples, own...  23.7 us
    unnamed x14, local copies, waits for them, and re-layouts  2.61 us
    pallas_call x1, Pallas kernels, on_device(): pl.pallas_call(store_kernel, out_shape=tuple((jax.ShapeDtypeStruct(r.shap...  0.86 us

profile of v2, /device:TPU:0, one launch (start us, length us, event | category | flops | bytes accessed | tf_op | source)
XLA Modules:
  0.0 27.9 jit_solution(1329948966449646678)
XLA Ops:
  0.6 0.0 copy-start.4
  0.6 0.0 copy-start.5
  0.7 0.0 copy-start.6
  0.7 0.0 copy-start.2
  0.7 0.0 copy-start.3
  0.7 0.6 %copy-done.4 = bf16[1,32]{1,0:T(2,128)(2,1)S(1)} copy-done((bf16[1,32]{1,0:T(2,128)(2,1)S(1)}, bf16[1,32]{1,0:T(2,128)(2,1)}, u32[]{:S(2)}) %copy-start.4) | copy-done | bytes 88
  1.3 0.0 copy-done.5
  1.3 0.0 copy-done.6
  1.3 0.0 copy-done.2
  1.4 0.0 copy-done.3
  1.4 0.0 copy-start
  1.4 1.0 %copy-done = bf16[1,8,256,128]{3,2,1,0:T(8,128)(2,1)S(1)} copy-done((bf16[1,8,256,128]{3,2,1,0:T(8,128)(2,1)S(1)}, bf16[1,8,256,128]{3,2,1,0:T(8,128)(2,1)}, u32[]{:S(2)}) %copy-start) | copy-done | bytes 524312
  2.4 0.0 copy-start.1
  2.4 0.9 %copy-done.1 = bf16[1152,32]{0,1:T(8,128)(2,1)S(1)} copy-done((bf16[1152,32]{0,1:T(8,128)(2,1)S(1)}, bf16[1152,32]{0,1:T(8,128)(2,1)}, u32[]{:S(2)}) %copy-start.1) | copy-done | bytes 73752
  3.3 23.7 %shard_map.110 = (f32[32,144]{1,0:T(8,128)S(1)}, f32[1,32]{1,0:T(1,128)S(1)}, f32[2,32]{1,0:T(2,128)S(1)}, f32[1,2]{1,0:T(1,128)S(1)}, bf16[2048,128]{1,0:T(8,128)(2,1)S(1)}) custom-call(bf16[2048,128]{1,0:T(8,128)(2,1)S(1)} %bitcast.8, s32[2,8]{1,0:T(2,128)S(1)} %bitcast.10, s32[1,8]{1,0:T(1,128)S(1)} %copy-done.3, bf16[32,1152]{1,0:T(8,128)(2,1)S(1)} %bitcast.9, ...), custom_call_target="tpu_custom_call" | custom-call | flops 1811939328 | bytes 1048576 | tf_op jit(solution)/shard_map/pallas_call | solution.py:363
  27.0 0.9 %shard_map.111 = (f32[32,144]{1,0:T(8,128)}, f32[1,32]{1,0:T(1,128)}, f32[2,32]{1,0:T(2,128)}, f32[1,2]{1,0:T(1,128)}, bf16[2048,128]{1,0:T(8,128)(2,1)}) custom-call(f32[32,144]{1,0:T(8,128)S(1)} %get-tuple-element.15.refs_0_, f32[1,32]{1,0:T(1,128)S(1)} %get-tuple-element.16.refs_1_, f32[2,32]{1,0:T(2,128)S(1)} %get-tuple-element.17.refs_2_, ...), custom_call_target="tpu_custom_call" | custom-call | tf_op jit(solution)/shard_map/pallas_call | solution.py:416
Async XLA Ops:
  0.6 0.7 %copy-start.4 = (bf16[1,32]{1,0:T(2,128)(2,1)S(1)}, bf16[1,32]{1,0:T(2,128)(2,1)}, u32[]{:S(2)}) copy-start(bf16[1,32]{1,0:T(2,128)(2,1)} %cb_ref.1) | copy-start | bytes 196
  0.6 0.7 %copy-start.5 = (bf16[2,32]{1,0:T(2,128)(2,1)S(1)}, bf16[2,32]{1,0:T(2,128)(2,1)}, u32[]{:S(2)}) copy-start(bf16[2,32]{1,0:T(2,128)(2,1)} %hw_ref.1) | copy-start | bytes 388
  0.7 0.7 %copy-start.6 = (f32[2]{0:T(128)S(1)}, f32[2]{0:T(128)}, u32[]{:S(2)}) copy-start(f32[2]{0:T(128)} %hb_ref.1) | copy-start | bytes 28
  0.7 0.7 %copy-start.2 = (s32[1,8,2]{1,2,0:T(2,128)S(1)}, s32[1,8,2]{1,2,0:T(2,128)}, u32[]{:S(2)}) copy-start(s32[1,8,2]{1,2,0:T(2,128)} %param.8) | copy-start | bytes 196
  0.7 0.7 %copy-start.3 = (s32[1,8]{1,0:T(1,128)S(1)}, s32[1,8]{1,0:T(1,128)}, u32[]{:S(2)}) copy-start(s32[1,8]{1,0:T(1,128)} %good_ref.1) | copy-start | bytes 100
  1.4 1.0 %copy-start = (bf16[1,8,256,128]{3,2,1,0:T(8,128)(2,1)S(1)}, bf16[1,8,256,128]{3,2,1,0:T(8,128)(2,1)}, u32[]{:S(2)}) copy-start(bf16[1,8,256,128]{3,2,1,0:T(8,128)(2,1)} %param.7) | copy-start | bytes 1572868
  2.4 0.9 %copy-start.1 = (bf16[1152,32]{0,1:T(8,128)(2,1)S(1)}, bf16[1152,32]{0,1:T(8,128)(2,1)}, u32[]{:S(2)}) copy-start(bf16[1152,32]{0,1:T(8,128)(2,1)} %param.10) | copy-start | bytes 221188

commit v3 on v2

--- a/solution.py
+++ b/solution.py
@@ -405,10 +405,10 @@
             flops=6 * cells * K9 * C, bytes_accessed=4 * cells * C, transcendentals=2 * cells * C
         ),
     )(
-        features.reshape(cells, C),
+        pltpu.with_memory_space_constraint(features.reshape(cells, C), pltpu.HBM),
         jnp.transpose(pick_index[0]),
         good_channel,
-        jnp.transpose(conv_weight),
+        pltpu.with_memory_space_constraint(jnp.transpose(conv_weight), pltpu.HBM),
         conv_bias,
         head_weight,
         head_bias,

time: 28.1 us -> 26.1 us (0.929)
  local copies, waits for them, and re-layouts: 2.61 us -> 0.69 us
    unnamed x14 -> x10, local copies, waits for them, and re-layouts: 2.61 us -> 0.69 us
where the time goes in v3:
time: 26.1 us; the launch traced here: 25.9 us
  Pallas kernels  24.6 us (94%)
  local copies, waits for them, and re-layouts  0.69 us (3%)
  between operations  0.68 us (3%)
    pallas_call x1, Pallas kernels, on_device(): pl.pallas_call(functools.partial(kernel, n_dp, n_fsdp, rows, samples, own...  23.7 us
    pallas_call x1, Pallas kernels, on_device(): pl.pallas_call(store_kernel, out_shape=tuple((jax.ShapeDtypeStruct(r.shap...  0.86 us
    unnamed x10, local copies, waits for them, and re-layouts  0.69 us

profile of v3, /device:TPU:0, one launch (start us, length us, event | category | flops | bytes accessed | tf_op | source)
XLA Modules:
  0.0 25.9 jit_solution(3033187249101873677)
XLA Ops:
  0.6 0.0 copy-start.2
  0.6 0.0 copy-start.3
  0.7 0.0 copy-start.4
  0.7 0.0 copy-start
  0.7 0.0 copy-start.1
  0.7 0.6 %copy-done.2 = bf16[1,32]{1,0:T(2,128)(2,1)S(1)} copy-done((bf16[1,32]{1,0:T(2,128)(2,1)S(1)}, bf16[1,32]{1,0:T(2,128)(2,1)}, u32[]{:S(2)}) %copy-start.2) | copy-done | bytes 88
  1.3 0.0 copy-done.3
  1.3 0.0 copy-done.4
  1.3 0.0 copy-done
  1.4 0.0 copy-done.1
  1.4 23.7 %shard_map.110 = (f32[32,144]{1,0:T(8,128)S(1)}, f32[1,32]{1,0:T(1,128)S(1)}, f32[2,32]{1,0:T(2,128)S(1)}, f32[1,2]{1,0:T(1,128)S(1)}, bf16[2048,128]{1,0:T(8,128)(2,1)S(1)}) custom-call(bf16[2048,128]{1,0:T(8,128)(2,1)} %bitcast.9, s32[2,8]{1,0:T(2,128)S(1)} %bitcast.8, s32[1,8]{1,0:T(1,128)S(1)} %copy-done.1, bf16[32,1152]{1,0:T(8,128)(2,1)} %bitcast.11, ...), custom_call_target="tpu_custom_call" | custom-call | flops 1811939328 | bytes 1048576 | tf_op jit(solution)/shard_map/pallas_call | solution.py:363
  25.1 0.9 %shard_map.111 = (f32[32,144]{1,0:T(8,128)}, f32[1,32]{1,0:T(1,128)}, f32[2,32]{1,0:T(2,128)}, f32[1,2]{1,0:T(1,128)}, bf16[2048,128]{1,0:T(8,128)(2,1)}) custom-call(f32[32,144]{1,0:T(8,128)S(1)} %get-tuple-element.15.refs_0_, f32[1,32]{1,0:T(1,128)S(1)} %get-tuple-element.16.refs_1_, f32[2,32]{1,0:T(2,128)S(1)} %get-tuple-element.17.refs_2_, ...), custom_call_target="tpu_custom_call" | custom-call | tf_op jit(solution)/shard_map/pallas_call | solution.py:416
Async XLA Ops:
  0.6 0.7 %copy-start.2 = (bf16[1,32]{1,0:T(2,128)(2,1)S(1)}, bf16[1,32]{1,0:T(2,128)(2,1)}, u32[]{:S(2)}) copy-start(bf16[1,32]{1,0:T(2,128)(2,1)} %cb_ref.1) | copy-start | bytes 196
  0.6 0.7 %copy-start.3 = (bf16[2,32]{1,0:T(2,128)(2,1)S(1)}, bf16[2,32]{1,0:T(2,128)(2,1)}, u32[]{:S(2)}) copy-start(bf16[2,32]{1,0:T(2,128)(2,1)} %hw_ref.1) | copy-start | bytes 388
  0.7 0.7 %copy-start.4 = (f32[2]{0:T(128)S(1)}, f32[2]{0:T(128)}, u32[]{:S(2)}) copy-start(f32[2]{0:T(128)} %hb_ref.1) | copy-start | bytes 28
  0.7 0.7 %copy-start = (s32[1,8,2]{1,2,0:T(2,128)S(1)}, s32[1,8,2]{1,2,0:T(2,128)}, u32[]{:S(2)}) copy-start(s32[1,8,2]{1,2,0:T(2,128)} %param.8) | copy-start | bytes 196
  0.7 0.7 %copy-start.1 = (s32[1,8]{1,0:T(1,128)S(1)}, s32[1,8]{1,0:T(1,128)}, u32[]{:S(2)}) copy-start(s32[1,8]{1,0:T(1,128)} %good_ref.1) | copy-start | bytes 100
